TPU v7x, 32 devices: a whole 2x2x4 slice. The times are simulated.
32 devices in a mesh: dp: 8 (over y, x, core), tensor: 4 (over z).
Axes of the slice: x: 2, y: 2, z: 4, core: 2. Of those that a mesh axis runs over, the one named last changes fastest.
Arguments:
- inputs: bfloat16 [32768, 768], P(('dp', 'tensor')), may hold values from -6 to 6
- encoded: bfloat16 [32768, 768], P(('dp', 'tensor')), may hold values from -6 to 6
- cotangent: bfloat16 [32768, 768], P(('dp', 'tensor')), may hold values from -6 to 6
- tgt_seg: int32 [32, 1024], P('dp'), may hold values from 0 to 4, as said below
- src_seg: int32 [32, 1024], P('dp'), may hold values from 0 to 4, as said below
- self_qkv: bfloat16 [3, 768, 768], P(None, None, 'tensor'), may hold values from -0.21875 to 0.21875
- self_out: bfloat16 [768, 768], P('tensor'), may hold values from -1.75 to 1.75
- cross_q: bfloat16 [768, 768], P(None, 'tensor'), may hold values from -0.21875 to 0.21875
- cross_kv: bfloat16 [2, 768, 768], P(None, None, 'tensor'), may hold values from -0.21875 to 0.21875
- cross_out: bfloat16 [768, 768], P('tensor'), may hold values from -1.75 to 1.75
- ffn_up: bfloat16 [768, 3072], P(None, 'tensor'), may hold values from -0.21875 to 0.21875
- ffn_down: bfloat16 [3072, 768], P('tensor'), may hold values from -0.109375 to 0.109375
- gains: float32 [3, 768], replicated, may hold values from 0.5 to 1.5
- shifts: float32 [3, 768], replicated, may hold values from -3 to 3
Outputs:
- layer_out: bfloat16 [32768, 768], P(('dp', 'tensor'))
- grad_inputs: bfloat16 [32768, 768], P(('dp', 'tensor'))
- grad_encoded: bfloat16 [32768, 768], P(('dp', 'tensor'))
- grad_self_qkv: float32 [3, 768, 768], P(None, None, 'tensor')
- grad_self_out: float32 [768, 768], P('tensor')
- grad_cross_q: float32 [768, 768], P(None, 'tensor')
- grad_cross_kv: float32 [2, 768, 768], P(None, None, 'tensor')
- grad_cross_out: float32 [768, 768], P('tensor')
- grad_ffn_up: float32 [768, 3072], P(None, 'tensor')
- grad_ffn_down: float32 [3072, 768], P('tensor')
- grad_gains: float32 [3, 768], replicated
- grad_shifts: float32 [3, 768], replicated
Inputs may be any that keep to these rules, and one draw needn't show every extreme that they name: `tgt_seg`: along each row the ids never fall; every id from 0 to 4 occurs in every row, and 4 marks the 1 to 128 padding positions at the row's end. `src_seg`: along each row the ids never fall; every id from 0 to 4 occurs in every row, and 4 marks the 1 to 128 padding positions at the row's end.
All inputs are finite; a program needn't handle non-finite values.
Results may differ from a plain program's by a relative error of at most 0.028.
Values may be sent and summed in bfloat16 or wider, within the bound.
A program may use at most 256 MiB of HBM per device.

v0:
```python
from functools import partial

import jax
import jax.numpy as jnp
from jax import lax
from jax.sharding import PartitionSpec as P

HDIM = 64


MASKED = -1e30
EPSILON = 1e-05


def norm_forward(summed, gain, shift):
    centred = summed - jnp.mean(summed, axis=-1, keepdims=True)
    inverse = lax.rsqrt(jnp.mean(centred * centred, axis=-1, keepdims=True) + EPSILON)
    normed = centred * inverse
    return (normed * gain + shift, normed, inverse)


def norm_backward(upstream, normed, inverse, gain):
    scaled = upstream * gain
    first_mean = jnp.mean(scaled, axis=-1, keepdims=True)
    second_mean = jnp.mean(scaled * normed, axis=-1, keepdims=True)
    result = inverse * (scaled - first_mean - normed * second_mean)
    return (result, jnp.sum(upstream * normed, axis=0), jnp.sum(upstream, axis=0))


def rows_times(left, weight, start, count):
    return jnp.dot(left, weight, preferred_element_type=jnp.float32)


def rows_times_t(left, weight, start, count):
    return lax.dot_general(
        left, weight, (((1,), (1,)), ((), ())), preferred_element_type=jnp.float32
    )


def stacked_back(stacked, weight, start, count):
    return jnp.einsum("cte,cde->td", stacked, weight, preferred_element_type=jnp.float32)


def contract_rows(left, right):
    return lax.dot_general(
        left, right, (((0,), (0,)), ((), ())), preferred_element_type=jnp.float32
    )


def enter_rows(values):
    return lax.all_gather(values, "tensor", axis=0, tiled=True)


def leave_sum(term_fn, share):
    return lax.psum_scatter(
        term_fn(jnp.int32(0), share * lax.axis_size("tensor")),
        "tensor",
        scatter_dimension=0,
        tiled=True,
    )


def grads_back(upstream):
    return lax.all_gather(upstream, "tensor", axis=0, tiled=True)


def entry_sum(term_fn, share):
    return lax.psum_scatter(
        term_fn(jnp.int32(0), share * lax.axis_size("tensor")).astype(jnp.bfloat16),
        "tensor",
        scatter_dimension=0,
        tiled=True,
    ).astype(jnp.float32)


def block_scores(query, key, query_flat, key_flat, item_index, block, per_row, key_len, causal):
    heads = query.shape[1] // HDIM
    row_index = item_index // per_row
    query_block = lax.dynamic_slice_in_dim(query, item_index * block, block, 0).reshape(
        block, heads, HDIM
    )
    key_row = lax.dynamic_slice_in_dim(key, row_index * key_len, key_len, 0).reshape(
        key_len, heads, HDIM
    )
    scores = jnp.einsum(
        "qhe,khe->hqk", query_block, key_row, preferred_element_type=jnp.float32
    ) * HDIM ** (-0.5)
    query_marks = lax.dynamic_slice_in_dim(query_flat, item_index * block, block, 0)
    key_marks = lax.dynamic_slice_in_dim(key_flat, row_index * key_len, key_len, 0)
    allowed = query_marks[:, None] == key_marks[None, :]
    if causal:
        offset = item_index % per_row * block
        allowed = allowed & (jnp.arange(key_len)[None, :] <= offset + jnp.arange(block)[:, None])
    return (jnp.where(allowed[None], scores, MASKED), query_block, key_row, row_index)


def attend(query, key, value, query_ids, key_ids, causal):
    block = min(512, query_ids.shape[1])
    per_row = query_ids.shape[1] // block
    key_len = key_ids.shape[1]
    heads = query.shape[1] // HDIM
    query_flat = query_ids.reshape(-1)
    key_flat = key_ids.reshape(-1)

    def one_block(item_index):
        scores, query_block, key_row, row_index = block_scores(
            query, key, query_flat, key_flat, item_index, block, per_row, key_len, causal
        )
        value_row = lax.dynamic_slice_in_dim(value, row_index * key_len, key_len, 0).reshape(
            key_len, heads, HDIM
        )
        largest = jnp.max(scores, axis=-1, keepdims=True)
        expanded = jnp.exp(scores - largest)
        summed = jnp.sum(expanded, axis=-1, keepdims=True)
        probs = (expanded / summed).astype(jnp.bfloat16)
        mixed = jnp.einsum("hqk,khe->qhe", probs, value_row, preferred_element_type=jnp.float32)
        return (
            mixed.reshape(block, heads * HDIM).astype(jnp.bfloat16),
            (largest + jnp.log(summed))[..., 0],
        )

    item_count = query.shape[0] // block
    mixed, log_totals = lax.map(one_block, jnp.arange(item_count, dtype=jnp.int32))
    return (mixed.reshape(query.shape[0], query.shape[1]), log_totals)


def attend_back(query, key, value, mixed_grad, log_totals, query_ids, key_ids, causal):
    block = min(512, query_ids.shape[1])
    per_row = query_ids.shape[1] // block
    key_len = key_ids.shape[1]
    heads = query.shape[1] // HDIM
    query_flat = query_ids.reshape(-1)
    key_flat = key_ids.reshape(-1)

    def one_block(carried, item_index):
        key_total, value_total = carried
        scores, query_block, key_row, row_index = block_scores(
            query, key, query_flat, key_flat, item_index, block, per_row, key_len, causal
        )
        value_row = lax.dynamic_slice_in_dim(value, row_index * key_len, key_len, 0).reshape(
            key_len, heads, HDIM
        )
        probs = jnp.exp(scores - log_totals[item_index][..., None])
        out_grad = lax.dynamic_slice_in_dim(mixed_grad, item_index * block, block, 0).reshape(
            block, heads, HDIM
        )
        prob_grad = jnp.einsum(
            "qhe,khe->hqk", out_grad, value_row, preferred_element_type=jnp.float32
        )
        score_grad = probs * (prob_grad - jnp.sum(probs * prob_grad, axis=-1, keepdims=True))
        score_grad = score_grad.astype(jnp.bfloat16)
        query_part = jnp.einsum(
            "hqk,khe->qhe", score_grad, key_row, preferred_element_type=jnp.float32
        ) * HDIM ** (-0.5)
        key_part = jnp.einsum(
            "hqk,qhe->khe", score_grad, query_block, preferred_element_type=jnp.float32
        ) * HDIM ** (-0.5)
        value_part = jnp.einsum(
            "hqk,qhe->khe", probs.astype(jnp.bfloat16), out_grad, preferred_element_type=jnp.float32
        )
        row_start = row_index * key_len
        key_sum = lax.dynamic_slice_in_dim(key_total, row_start, key_len, 0) + key_part.reshape(
            key_len, heads * HDIM
        )
        value_sum = lax.dynamic_slice_in_dim(
            value_total, row_start, key_len, 0
        ) + value_part.reshape(key_len, heads * HDIM)
        key_total = lax.dynamic_update_slice_in_dim(key_total, key_sum, row_start, 0)
        value_total = lax.dynamic_update_slice_in_dim(value_total, value_sum, row_start, 0)
        return (
            (key_total, value_total),
            query_part.reshape(block, heads * HDIM).astype(jnp.bfloat16),
        )

    empty = jnp.zeros(key.shape, jnp.float32)
    item_count = query.shape[0] // block
    (key_total, value_total), query_grad = lax.scan(
        one_block, (empty, empty), jnp.arange(item_count, dtype=jnp.int32)
    )
    return (
        query_grad.reshape(query.shape[0], query.shape[1]),
        key_total.astype(jnp.bfloat16),
        value_total.astype(jnp.bfloat16),
    )


def per_device(
    inputs,
    encoded,
    cotangent,
    tgt_seg,
    src_seg,
    self_qkv,
    self_out,
    cross_q,
    cross_kv,
    cross_out,
    ffn_up,
    ffn_down,
    gains,
    shifts,
):
    self_weight, self_back, cross_weight, pair_weight = (self_qkv, self_out, cross_q, cross_kv)
    cross_back, up_weight, down_weight = (cross_out, ffn_up, ffn_down)
    target_rows, source_rows = (
        lax.all_gather(inputs, "tensor", axis=0, tiled=True),
        lax.all_gather(encoded, "tensor", axis=0, tiled=True),
    )
    target_ids, source_ids = (tgt_seg, src_seg)
    share = inputs.shape[0]
    projected = jnp.einsum(
        "td,cde->cte", target_rows, self_weight, preferred_element_type=jnp.float32
    )
    projected = projected.astype(jnp.bfloat16)
    self_mixed, self_totals = attend(
        projected[0], projected[1], projected[2], target_ids, target_ids, True
    )
    summed = inputs.astype(jnp.float32) + leave_sum(
        partial(rows_times, self_mixed, self_back), share
    )
    first_out, first_normed, first_inverse = norm_forward(summed, gains[0], shifts[0])
    first_rows = enter_rows(first_out.astype(jnp.bfloat16))
    cross_query = jnp.dot(first_rows, cross_weight, preferred_element_type=jnp.float32).astype(
        jnp.bfloat16
    )
    cross_pairs = jnp.einsum(
        "sd,cde->cse", source_rows, pair_weight, preferred_element_type=jnp.float32
    )
    cross_pairs = cross_pairs.astype(jnp.bfloat16)
    cross_mixed, cross_totals = attend(
        cross_query, cross_pairs[0], cross_pairs[1], target_ids, source_ids, False
    )
    summed = first_out + leave_sum(partial(rows_times, cross_mixed, cross_back), share)
    second_out, second_normed, second_inverse = norm_forward(summed, gains[1], shifts[1])
    second_rows = enter_rows(second_out.astype(jnp.bfloat16))
    hidden_pre = jnp.dot(second_rows, up_weight, preferred_element_type=jnp.float32)
    hidden = jax.nn.gelu(hidden_pre, approximate=False).astype(jnp.bfloat16)
    summed = second_out + leave_sum(partial(rows_times, hidden, down_weight), share)
    third_out, third_normed, third_inverse = norm_forward(summed, gains[2], shifts[2])
    layer_out = third_out.astype(jnp.bfloat16)
    third_grad, third_gain, third_shift = norm_backward(
        cotangent.astype(jnp.float32), third_normed, third_inverse, gains[2]
    )
    branch_grad = grads_back(third_grad.astype(jnp.bfloat16))
    grad_down = contract_rows(hidden, branch_grad)
    hidden_grad = lax.dot_general(
        branch_grad, down_weight, (((1,), (1,)), ((), ())), preferred_element_type=jnp.float32
    )
    gelu_value, gelu_pull = jax.vjp(partial(jax.nn.gelu, approximate=False), hidden_pre)
    up_grad = gelu_pull(hidden_grad)[0].astype(jnp.bfloat16)
    grad_up = contract_rows(second_rows, up_grad)
    second_grad = third_grad + entry_sum(partial(rows_times_t, up_grad, up_weight), share)
    second_grad, second_gain, second_shift = norm_backward(
        second_grad, second_normed, second_inverse, gains[1]
    )
    branch_grad = grads_back(second_grad.astype(jnp.bfloat16))
    grad_cross_out = contract_rows(cross_mixed, branch_grad)
    mixed_grad = lax.dot_general(
        branch_grad, cross_back, (((1,), (1,)), ((), ())), preferred_element_type=jnp.float32
    ).astype(jnp.bfloat16)
    query_grad, key_grad, value_grad = attend_back(
        cross_query,
        cross_pairs[0],
        cross_pairs[1],
        mixed_grad,
        cross_totals,
        target_ids,
        source_ids,
        False,
    )
    pair_grad = jnp.stack([key_grad, value_grad])
    grad_cross_q = contract_rows(first_rows, query_grad)
    grad_cross_kv = jnp.einsum(
        "sd,cse->cde", source_rows, pair_grad, preferred_element_type=jnp.float32
    )
    grad_encoded = entry_sum(
        partial(stacked_back, pair_grad, pair_weight), encoded.shape[0]
    ).astype(jnp.bfloat16)
    first_grad = second_grad + entry_sum(partial(rows_times_t, query_grad, cross_weight), share)
    first_grad, first_gain, first_shift = norm_backward(
        first_grad, first_normed, first_inverse, gains[0]
    )
    branch_grad = grads_back(first_grad.astype(jnp.bfloat16))
    grad_self_out = contract_rows(self_mixed, branch_grad)
    mixed_grad = lax.dot_general(
        branch_grad, self_back, (((1,), (1,)), ((), ())), preferred_element_type=jnp.float32
    ).astype(jnp.bfloat16)
    query_grad, key_grad, value_grad = attend_back(
        projected[0],
        projected[1],
        projected[2],
        mixed_grad,
        self_totals,
        target_ids,
        target_ids,
        True,
    )
    projected_grad = jnp.stack([query_grad, key_grad, value_grad])
    grad_self_qkv = jnp.einsum(
        "td,cte->cde", target_rows, projected_grad, preferred_element_type=jnp.float32
    )
    grad_inputs = first_grad + entry_sum(partial(stacked_back, projected_grad, self_weight), share)
    grad_inputs = grad_inputs.astype(jnp.bfloat16)
    totals = lax.psum(
        (
            grad_self_qkv,
            grad_self_out,
            grad_cross_q,
            grad_cross_kv,
            grad_cross_out,
            grad_up,
            grad_down,
        ),
        "dp",
    )
    grad_gains, grad_shifts = lax.psum(
        (
            jnp.stack([first_gain, second_gain, third_gain]),
            jnp.stack([first_shift, second_shift, third_shift]),
        ),
        ("dp", "tensor"),
    )
    return (
        layer_out,
        grad_inputs,
        grad_encoded,
        totals[0],
        totals[1],
        totals[2],
        totals[3],
        totals[4],
        totals[5],
        totals[6],
        grad_gains,
        grad_shifts,
    )


def solution(mesh):
    in_specs = (
        P(("dp", "tensor"), None),
        P(("dp", "tensor"), None),
        P(("dp", "tensor"), None),
        P("dp", None),
        P("dp", None),
        P(None, None, "tensor"),
        P("tensor", None),
        P(None, "tensor"),
        P(None, None, "tensor"),
        P("tensor", None),
        P(None, "tensor"),
        P("tensor", None),
        P(),
        P(),
    )
    out_specs = (
        P(("dp", "tensor"), None),
        P(("dp", "tensor"), None),
        P(("dp", "tensor"), None),
        P(None, None, "tensor"),
        P("tensor", None),
        P(None, "tensor"),
        P(None, None, "tensor"),
        P("tensor", None),
        P(None, "tensor"),
        P("tensor", None),
        P(),
        P(),
    )
    return jax.shard_map(
        per_device, mesh=mesh, in_specs=in_specs, out_specs=out_specs, check_vma=False
    )
```

profile of v0, /device:TPU:0, one launch (start us, length us, event | category | flops | bytes accessed | tf_op | source)
XLA Modules:
  0.0 2943.7 jit_solution(9901902736314340096)
XLA Ops:
  8.7 119.0 %all-gather.8.cloned.1.call-done = bf16[4096,768]{1,0:T(8,128)(2,1)} async-done(((bf16[1024,768]{1,0:T(8,128)(2,1)}), bf16[4096,768]{1,0:T(8,128)(2,1)}) %all-gather.8.cloned.1.call-update) | async-done | bytes 6291472 | tf_op jit(solution)/shard_map/all_gather | solution.py:206
  138.6 119.9 %while.62 = (s32[]{:T(128)}, bf16[8,512,192]{1,2,0:T(8,128)(2,1)}, f32[8,3,512]{2,1,0:T(4,128)}, s32[8]{0:T(128)S(1)}, bf16[4096,192]{0,1:T(8,128)(2,1)}, /*inde...) while((s32[]{:T(128)}, bf16[8,512,192]{1,2,0:T(8,128)(2,1)}, ...), condition=%wide.region_3.4_spmd, body=%wide.region_0.3_spmd.sunk | while | flops 423197728 | bytes 24585992 | solution.py:123
  269.9 208.8 %reduce-scatter.8.cloned.1.call-done = f32[1024,768]{1,0:T(8,128)} async-done(((f32[4096,768]{1,0:T(8,128)}), f32[1024,768]{1,0:T(8,128)}) %reduce-scatter.8.cloned.1.call-update) | async-done | bytes 3145744 | tf_op jit(solution)/shard_map/reduce_scatter | solution.py:55
  485.3 111.4 %all-gather.10.cloned.1.call-done = bf16[4096,768]{1,0:T(8,128)(2,1)} async-done(((bf16[1024,768]{1,0:T(8,128)(2,1)}), bf16[4096,768]{1,0:T(8,128)(2,1)}) %all-gather.10.cloned.1.call-update) | async-done | bytes 6291472 | tf_op jit(solution)/shard_map/all_gather | solution.py:207
  605.3 107.0 %all-gather.12.cloned.1.call-done = bf16[4096,768]{1,0:T(8,128)(2,1)} async-done(((bf16[1024,768]{1,0:T(8,128)(2,1)}), bf16[4096,768]{1,0:T(8,128)(2,1)}) %all-gather.12.cloned.1.call-update) | async-done | bytes 6291472 | tf_op jit(solution)/shard_map/all_gather | solution.py:51
  720.3 115.3 %while.63 = (s32[]{:T(128)}, bf16[8,512,192]{1,2,0:T(8,128)(2,1)}, f32[8,3,512]{2,1,0:T(4,128)}, s32[8]{0:T(128)S(1)}, bf16[4096,192]{0,1:T(8,128)(2,1)}, /*inde...) while((s32[]{:T(128)}, bf16[8,512,192]{1,2,0:T(8,128)(2,1)}, ...), condition=%wide.region_10.11_spmd, body=%wide.region_7.10_spmd.sunk | while | flops 422148640 | bytes 24581844 | solution.py:123
  845.5 210.2 %reduce-scatter.10.cloned.1.call-done = f32[1024,768]{1,0:T(8,128)} async-done(((f32[4096,768]{1,0:T(8,128)}), f32[1024,768]{1,0:T(8,128)}) %reduce-scatter.10.cloned.1.call-update) | async-done | bytes 3145744 | tf_op jit(solution)/shard_map/reduce_scatter | solution.py:55
  1062.9 11.0 reduce-scatter.12.cloned.1.call-start
  1073.9 105.5 %all-gather.14.cloned.1.call-done = bf16[4096,768]{1,0:T(8,128)(2,1)} async-done(((bf16[1024,768]{1,0:T(8,128)(2,1)}), bf16[4096,768]{1,0:T(8,128)(2,1)}) %all-gather.14.cloned.1.call-update) | async-done | bytes 6291472 | tf_op jit(solution)/shard_map/all_gather | solution.py:51
  1179.4 33.5 %multiply_convert_fusion.2 = (bf16[4096,768]{1,0:T(8,128)(2,1)S(1)}, f32[4096,768]{1,0:T(8,128)}, f32[4096,768]{1,0:T(8,128)}) fusion(bf16[4096,768]{1,0:T(8,128)(2,1)} %all-gather.14.cloned.1.call-done, bf16[768,768]{1,0:T(8,128)(2,1)S(1)} %copy-done), kind=kOutput, calls=%fused_computation.83 | convolution fusion | flops 5036310528 | bytes 38928384 | tf_op jit(solution)/shard_map/dot_general | solution.py:236
  1223.7 210.2 %reduce-scatter.12.cloned.1.call-done = f32[1024,768]{1,0:T(8,128)} async-done(((f32[4096,768]{1,0:T(8,128)}), f32[1024,768]{1,0:T(8,128)}) %reduce-scatter.12.cloned.1.call-update) | async-done | bytes 3145744 | tf_op jit(solution)/shard_map/reduce_scatter | solution.py:55
  1444.9 116.5 %all-gather.16.cloned.1.call-done = bf16[4096,768]{1,0:T(8,128)(2,1)} async-done(((bf16[1024,768]{1,0:T(8,128)(2,1)}), bf16[4096,768]{1,0:T(8,128)(2,1)}) %all-gather.16.cloned.1.call-update) | async-done | bytes 6291472 | tf_op jit(solution)/shard_map/all_gather | solution.py:64
  1561.4 17.0 add_convert_fusion
  1588.2 109.1 %reduce-scatter.14.cloned.1.call-done = bf16[1024,768]{1,0:T(8,128)(2,1)} async-done(((bf16[4096,768]{1,0:T(8,128)(2,1)}), bf16[1024,768]{1,0:T(8,128)(2,1)}) %reduce-scatter.14.cloned.1.call-update) | async-done | bytes 1572880 | tf_op jit(solution)/shard_map/reduce_scatter | solution.py:68
  1706.2 115.6 %all-gather.18.cloned.1.call-done = bf16[4096,768]{1,0:T(8,128)(2,1)} async-done(((bf16[1024,768]{1,0:T(8,128)(2,1)}), bf16[4096,768]{1,0:T(8,128)(2,1)}) %all-gather.18.cloned.1.call-update) | async-done | bytes 6291472 | tf_op jit(solution)/shard_map/all_gather | solution.py:64
  1832.1 226.0 %while.64 = (s32[]{:T(128)}, f32[4096,192]{0,1:T(8,128)}, f32[4096,192]{0,1:T(8,128)}, bf16[8,512,192]{1,2,0:T(8,128)(2,1)S(1)}, s32[8]{0:T(128)S(1)}, /*index=5...) while((s32[]{:T(128)}, f32[4096,192]{0,1:T(8,128)}, ...), condition=%wide.region_24.25_spmd, body=%wide.region_22.24_spmd.sunk | while | flops 1031535104 | bytes 79426064 | solution.py:177
  2065.5 109.1 %reduce-scatter.16.cloned.1.call-done = bf16[1024,768]{1,0:T(8,128)(2,1)} async-done(((bf16[4096,768]{1,0:T(8,128)(2,1)}), bf16[1024,768]{1,0:T(8,128)(2,1)}) %reduce-scatter.16.cloned.1.call-update) | async-done | bytes 1572880 | tf_op jit(solution)/shard_map/reduce_scatter | solution.py:68
  2183.1 116.0 %all-gather.20.cloned.1.call-done = bf16[4096,768]{1,0:T(8,128)(2,1)} async-done(((bf16[1024,768]{1,0:T(8,128)(2,1)}), bf16[4096,768]{1,0:T(8,128)(2,1)}) %all-gather.20.cloned.1.call-update) | async-done | bytes 6291472 | tf_op jit(solution)/shard_map/all_gather | solution.py:64
  2310.5 227.0 %while.65 = (s32[]{:T(128)}, f32[4096,192]{0,1:T(8,128)}, f32[4096,192]{0,1:T(8,128)}, bf16[8,512,192]{1,2,0:T(8,128)(2,1)}, s32[8]{0:T(128)S(1)}, /*index=5*/bf...) while((s32[]{:T(128)}, f32[4096,192]{0,1:T(8,128)}, ...), condition=%wide.region_30.31_spmd, body=%wide.region_28.30_spmd.sunk | while | flops 1032584192 | bytes 79430720 | solution.py:177
  2567.2 10.2 fusion.95
  2604.7 45.4 %all-reduce = (f32[3,768]{1,0:T(4,128)}, f32[3,768]{1,0:T(4,128)}) all-reduce(f32[3,768]{1,0:T(4,128)S(1)} %pad_maximum_fusion.10, f32[3,768]{1,0:T(4,128)S(1)} %pad_maximum_fusion.11), channel_id=1, replica_groups=mesh['dp'=8,'tensor'=4] {'dp','tensor'}, use_global_device_ids=true, to_apply=%region_43.44 | all-reduce | flops 4608 | bytes 36864 | tf_op jit(solution)/shard_map/psum | solution.py:316
  2650.2 16.8 reduce-scatter.18.cloned.1.call-done
  2670.8 110.2 %reduce-scatter.20.cloned.1.call-done = bf16[1024,768]{1,0:T(8,128)(2,1)} async-done(((bf16[4096,768]{1,0:T(8,128)(2,1)}), bf16[1024,768]{1,0:T(8,128)(2,1)}) %reduce-scatter.20.cloned.1.call-update) | async-done | bytes 1572880 | tf_op jit(solution)/shard_map/reduce_scatter | solution.py:68
  2781.0 146.6 %all-reduce.4.cloned.1.call-done = (f32[3,768,192]{1,2,0:T(8,128)}, f32[192,768]{1,0:T(8,128)}, f32[768,192]{0,1:T(8,128)}, f32[2,768,192]{1,2,0:T(8,128)}, f32[...) async-done(((f32[3,768,192]{1,2,0:T(8,128)}, f32[192,768]{1,0:T(8,128)}, f32[768,192]{0,1:T(8,128)}, f32[2,768,192]{1,2,0:T(8,128)}, f32[192,768]{1,0:T(8,128)}, ...) | async-done | bytes 9437200 | tf_op jit(solution)/shard_map/psum | solution.py:304
  (898 shorter events, 775.6 us)
Async XLA Ops:
  7.2 1172.3 %copy-start = (bf16[768,768]{1,0:T(8,128)(2,1)S(1)}, bf16[768,768]{1,0:T(8,128)(2,1)}, u32[]{:S(2)}) copy-start(bf16[768,768]{1,0:T(8,128)(2,1)} %param.32) | copy-start | bytes 3538948
  7.2 120.5 %all-gather.8.cloned.1.call-start = ((), (), s32[]{:S(2)}) async-start(), calls=%async_computation.7 | async-start | bytes 7864320 | tf_op jit(solution)/shard_map/all_gather | solution.py:206
  7.9 470.7 %reduce-scatter.8.cloned.1.call-start = ((), (), s32[]{:S(2)}) async-start(), calls=%async_computation.8 | async-start | bytes 15728640 | tf_op jit(solution)/shard_map/reduce_scatter | solution.py:55
  268.4 210.3 %copy-start.16 = (bf16[1024,768]{1,0:T(8,128)(2,1)S(1)}, bf16[1024,768]{1,0:T(8,128)(2,1)}, u32[]{:S(2)}) copy-start(bf16[1024,768]{1,0:T(8,128)(2,1)} %param.22) | copy-start | bytes 4718596
  268.4 328.3 %all-gather.10.cloned.1.call-start = ((), (), s32[]{:S(2)}) async-start(), calls=%async_computation.9 | async-start | bytes 7864320 | tf_op jit(solution)/shard_map/all_gather | solution.py:207
  269.2 443.1 %all-gather.12.cloned.1.call-start = ((), (), s32[]{:S(2)}) async-start(), calls=%async_computation.10 | async-start | bytes 7864320 | tf_op jit(solution)/shard_map/all_gather | solution.py:51
  269.9 211.6 %copy-start.51 = (f32[768]{0:T(1024)}, f32[768]{0:T(1024)S(1)}, u32[]{:S(2)}) copy-start(f32[768]{0:T(1024)S(1)} %get-tuple-element.731) | copy-start | bytes 9220
  269.9 211.6 %copy-start.56 = (f32[768]{0:T(1024)}, f32[768]{0:T(1024)S(1)}, u32[]{:S(2)}) copy-start(f32[768]{0:T(1024)S(1)} %get-tuple-element.602) | copy-start | bytes 9220
  484.4 571.3 %reduce-scatter.10.cloned.1.call-start = ((), (), s32[]{:S(2)}) async-start(), calls=%async_computation.11 | async-start | bytes 15728640 | tf_op jit(solution)/shard_map/reduce_scatter | solution.py:55
  845.4 210.3 %copy-start.46 = (f32[1024]{0:T(1024)S(1)}, f32[1024]{0:T(1024)}, u32[]{:S(2)}) copy-start(f32[1024]{0:T(1024)} %copy-done.45) | copy-start | bytes 12292
  845.4 210.3 %copy-start.49 = (f32[1024]{0:T(1024)S(1)}, f32[1024]{0:T(1024)}, u32[]{:S(2)}) copy-start(f32[1024]{0:T(1024)} %copy-done.48) | copy-start | bytes 12292
  845.4 210.3 %copy-start.52 = (f32[768]{0:T(1024)S(1)}, f32[768]{0:T(1024)}, u32[]{:S(2)}) copy-start(f32[768]{0:T(1024)} %copy-done.51) | copy-start | bytes 9220
  845.4 210.3 %copy-start.57 = (f32[768]{0:T(1024)S(1)}, f32[768]{0:T(1024)}, u32[]{:S(2)}) copy-start(f32[768]{0:T(1024)} %copy-done.56) | copy-start | bytes 9220
  845.4 334.0 %all-gather.14.cloned.1.call-start = ((), (), s32[]{:S(2)}) async-start(), calls=%async_computation.12 | async-start | bytes 7864320 | tf_op jit(solution)/shard_map/all_gather | solution.py:51
  1062.9 152.7 %copy-start.69 = (bf16[768,768]{1,0:T(8,128)(2,1)S(1)}, bf16[768,768]{1,0:T(8,128)(2,1)}, u32[]{:S(2)}) copy-start(bf16[768,768]{1,0:T(8,128)(2,1)} %param.33) | copy-start | bytes 3538948
  1062.9 371.1 %reduce-scatter.12.cloned.1.call-start = ((), (), s32[]{:S(2)}) async-start(), calls=%async_computation.13 | async-start | bytes 15728640 | tf_op jit(solution)/shard_map/reduce_scatter | solution.py:55
  1223.7 337.7 %all-gather.16.cloned.1.call-start = ((), (), s32[]{:S(2)}) async-start(), calls=%async_computation.14 | async-start | bytes 7864320 | tf_op jit(solution)/shard_map/all_gather | solution.py:64
  1444.9 252.4 %reduce-scatter.14.cloned.1.call-start = ((), (), s32[]{:S(2)}) async-start(), calls=%async_computation.15 | async-start | bytes 7864320 | tf_op jit(solution)/shard_map/reduce_scatter | solution.py:68
  1588.2 233.6 %all-gather.18.cloned.1.call-start = ((), (), s32[]{:S(2)}) async-start(), calls=%async_computation.16 | async-start | bytes 7864320 | tf_op jit(solution)/shard_map/all_gather | solution.py:64
  1705.7 468.9 %reduce-scatter.16.cloned.1.call-start = ((), (), s32[]{:S(2)}) async-start(), calls=%async_computation.17 | async-start | bytes 7864320 | tf_op jit(solution)/shard_map/reduce_scatter | solution.py:68
  2065.5 233.6 %all-gather.20.cloned.1.call-start = ((), (), s32[]{:S(2)}) async-start(), calls=%async_computation.18 | async-start | bytes 7864320 | tf_op jit(solution)/shard_map/all_gather | solution.py:64
  2183.0 483.9 %reduce-scatter.18.cloned.1.call-start = ((), (), s32[]{:S(2)}) async-start(), calls=%async_computation.19 | async-start | bytes 7864320 | tf_op jit(solution)/shard_map/reduce_scatter | solution.py:68
  2556.8 224.2 %reduce-scatter.20.cloned.1.call-start = ((), (), s32[]{:S(2)}) async-start(), calls=%async_computation.20 | async-start | bytes 7864320 | tf_op jit(solution)/shard_map/reduce_scatter | solution.py:68
  2567.1 360.5 %all-reduce.4.cloned.1.call-start = ((), (), s32[]{:S(2)}) async-start(), calls=%async_computation.21 | async-start | bytes 18874368 | tf_op jit(solution)/shard_map/psum | solution.py:304
  (139 other events, 1313.1 us)
Sparse Core Ops, SparseCore 0:
  9.6 118.0 all-gather.7
  268.5 210.0 reduce-scatter.7
  480.2 116.3 all-gather.9
  598.7 113.5 all-gather.11
  845.6 210.0 reduce-scatter.9
  1063.0 116.3 all-gather.13
  1223.8 210.0 reduce-scatter.11
  1445.0 116.3 all-gather.15
  1588.3 108.9 reduce-scatter.13
  1705.8 115.8 all-gather.17
  2065.6 108.9 reduce-scatter.15
  2183.1 115.8 all-gather.19
  2556.9 110.0 reduce-scatter.17
  2669.7 111.2 reduce-scatter.19
  2786.7 140.7 all-reduce.3
where the time goes:
time: 2960 us; the launch traced here: 2940 us
  waiting for transfers between devices  1910 us (65%)
  matrix products  420 us (14%)
  local copies, waits for them, and re-layouts  226 us (8%)
  other arithmetic  188 us (6%)
  loops' own time  124 us (4%)
  blocking collectives  45.4 us (2%)
    reduce_scatter x3, waiting for transfers between devices, leave_sum(): lax.psum_scatter(term_fn(jnp.int32(0), share * lax.axis_size('tensor')),...  629 us
    all_gather x3, waiting for transfers between devices, grads_back(): return lax.all_gather(upstream, 'tensor', axis=0, tiled=True)  348 us
    reduce_scatter x4, waiting for transfers between devices, entry_sum(): lax.psum_scatter(term_fn(jnp.int32(0), share * lax.axis_size('tensor')).a...  345 us
    all_gather x2, waiting for transfers between devices, enter_rows(): return lax.all_gather(values, 'tensor', axis=0, tiled=True)  213 us
    psum x1, waiting for transfers between devices, per_device(): lax.psum((grad_self_qkv, grad_self_out, grad_cross_q, grad_cross_kv, grad...  147 us
    all_gather x1, waiting for transfers between devices, per_device(): lax.all_gather(inputs, 'tensor', axis=0, tiled=True)  119 us
    all_gather x1, waiting for transfers between devices, per_device(): lax.all_gather(encoded, 'tensor', axis=0, tiled=True)  111 us
    dot_general x32, matrix products, block_scores(): jnp.einsum('qhe,khe->hqk', query_block, key_row, preferred_element_type=j...  80.6 us
  transfers between devices with their start and end apart: 15, of which 15 were waited for; matrix products, arithmetic and copies ran while one was open for 2% of the time, Pallas kernels for 0%

commit v1 on v0

v1 whole, which is shorter than its diff:
```python
import functools
import jax, jax.numpy as jnp
from jax import lax
from jax.sharding import PartitionSpec as P
from jax.experimental import pallas as pl
from jax.experimental.pallas import tpu as pltpu

HDIM = 64
LANES = 128
MASKED = -1e30
EPSILON = 1e-5
F32 = jnp.float32
BF16 = jnp.bfloat16
NT = (((1,), (1,)), ((), ()))
TN = (((0,), (0,)), ((), ()))
NN = (((1,), (0,)), ((), ()))


def dot(a, b, dims):
    return lax.dot_general(a, b, dims, preferred_element_type=F32)


def attend_kernel(causal, bq, bk, lo_ref, hi_ref, q_ref, k_ref, v_ref, fq_ref, fk_ref, o_ref, lse_ref):
    n = q_ref.shape[0]
    lane = lax.broadcasted_iota(jnp.int32, (bq, LANES), 1)
    first = lane < HDIM
    ones = jnp.ones((bk, LANES), BF16)
    for i in range(n // bq):
        rows = pl.ds(i * bq, bq)
        q = q_ref[rows, :] * jnp.asarray(HDIM ** -0.5, BF16)
        fq = fq_ref[rows, :]
        zero = jnp.zeros_like(q)
        qs = jnp.concatenate(
            [
                jnp.concatenate([jnp.where(first, q, zero), fq], axis=1),
                jnp.concatenate([jnp.where(first, zero, q), fq], axis=1),
            ],
            axis=0,
        )

        def step(j, carry, diagonal=False):
            top, acc = carry
            keys = pl.ds(pl.multiple_of(j * bk, bk), bk)
            ks = jnp.concatenate([k_ref[keys, :], fk_ref[keys, :]], axis=1)
            s = dot(qs, ks, NT)
            if diagonal:
                row = lax.broadcasted_iota(jnp.int32, (2 * bq, bk), 0)
                row = jnp.where(row >= bq, row - bq, row) + i * bq
                col = lax.broadcasted_iota(jnp.int32, (2 * bq, bk), 1) + j * bk
                s = jnp.where(col <= row, s, MASKED)
            new_top = jnp.maximum(top, jnp.max(s, axis=1, keepdims=True))
            p = jnp.exp(s - new_top).astype(BF16)
            vs = jnp.concatenate([v_ref[keys, :], ones], axis=1)
            acc = acc * jnp.exp(top - new_top) + dot(p, vs, NN)
            return new_top, acc

        carry = (jnp.full((2 * bq, 1), MASKED, F32), jnp.zeros((2 * bq, 2 * LANES), F32))
        if causal:
            diag = [i * bq // bk + d for d in range(max(1, bq // bk))]
            for j in diag:
                carry = step(j, carry, True)
            carry = lax.fori_loop(lo_ref[i], diag[0], step, carry)
        else:
            carry = lax.fori_loop(lo_ref[i], hi_ref[i], step, carry)
        top, acc = carry
        total = acc[:, LANES : LANES + 1]
        out = acc[:, :LANES] / total
        o_ref[rows, :] = jnp.where(first, out[:bq], out[bq:]).astype(BF16)
        lse = top + jnp.log(total)
        lse_ref[rows, :] = jnp.where(lane == 0, lse[:bq], lse[bq:])


def attend_back_kernel(
    causal, bq, bk, lo_ref, hi_ref, q_ref, k_ref, v_ref, fq_ref, fk_ref, g_ref, lse_ref, d_ref, dq_ref, dk_ref, dv_ref, dq_acc
):
    n = q_ref.shape[0]
    m = k_ref.shape[0]
    lane = lax.broadcasted_iota(jnp.int32, (bk, LANES), 1)
    first = lane < HDIM
    dq_acc[...] = jnp.zeros_like(dq_acc)
    scale = jnp.asarray(HDIM ** -0.5, BF16)
    for j in range(m // bk):
        keys = pl.ds(j * bk, bk)
        k = k_ref[keys, :]
        v = v_ref[keys, :]
        fk = fk_ref[keys, :]
        zero = jnp.zeros_like(k)
        kh = jnp.concatenate([jnp.where(first, k, zero), jnp.where(first, zero, k)], axis=0)
        ks = jnp.concatenate([kh, jnp.concatenate([fk, fk], axis=0)], axis=1)
        vs = jnp.concatenate([jnp.where(first, v, zero), jnp.where(first, zero, v)], axis=0)

        def step(i, carry, diagonal=False):
            dk, dv = carry
            rows = pl.ds(pl.multiple_of(i * bq, bq), bq)
            q = q_ref[rows, :] * scale
            qs = jnp.concatenate([q, fq_ref[rows, :]], axis=1)
            g = g_ref[rows, :]
            s = dot(ks, qs, NT)
            if diagonal:
                row = lax.broadcasted_iota(jnp.int32, (2 * bk, bq), 1) + i * bq
                col = lax.broadcasted_iota(jnp.int32, (2 * bk, bq), 0)
                col = jnp.where(col >= bk, col - bk, col) + j * bk
                s = jnp.where(col <= row, s, MASKED)
            lse = lse_ref[0, :, rows]
            delta = d_ref[0, :, rows]
            dp = dot(vs, g, NT)
            p0 = jnp.exp(s[:bk] - lse[0:1, :])
            p1 = jnp.exp(s[bk:] - lse[1:2, :])
            ds0 = (p0 * (dp[:bk] - delta[0:1, :])).astype(BF16)
            ds1 = (p1 * (dp[bk:] - delta[1:2, :])).astype(BF16)
            p = jnp.concatenate([p0.astype(BF16), p1.astype(BF16)], axis=0)
            ds = jnp.concatenate([ds0, ds1], axis=0)
            dv = dv + dot(p, g, NN)
            dk = dk + dot(ds, q, NN)
            dq_acc[rows, :] += dot(ds, kh, TN)
            return dk, dv

        carry = (jnp.zeros((2 * bk, LANES), F32), jnp.zeros((2 * bk, LANES), F32))
        if causal:
            diag = [j * bk // bq + d for d in range(max(1, bk // bq))]
            for i in diag:
                carry = step(i, carry, True)
            carry = lax.fori_loop(diag[-1] + 1, hi_ref[j], step, carry)
        else:
            carry = lax.fori_loop(lo_ref[j], hi_ref[j], step, carry)
        dk, dv = carry
        dk_ref[keys, :] = jnp.where(first, dk[:bk], dk[bk:]).astype(BF16)
        dv_ref[keys, :] = jnp.where(first, dv[:bk], dv[bk:]).astype(BF16)
    dq_ref[...] = (dq_acc[...] * HDIM ** -0.5).astype(BF16)


def block_range(own, other, block, other_block):
    own = own.reshape(-1, block)
    lo = jnp.sum((other[None, :] < own[:, :1]).astype(jnp.int32), axis=1) // other_block
    hi = jnp.sum((other[None, :] <= own[:, -1:]).astype(jnp.int32), axis=1)
    return lo, (hi + other_block - 1) // other_block


def seg_features(q_ids, k_ids):
    lanes = jnp.arange(LANES, dtype=jnp.int32)[None, :]
    fq = jnp.where((lanes < 5) & (q_ids[:, None] != lanes), MASKED, 0.0).astype(BF16)
    fk = (k_ids[:, None] == lanes).astype(BF16)
    return fq, fk


VMEM_LIMIT = 56 * 2**20


def attend(q, k, v, q_ids, k_ids, fq, fk, causal, bq=256, bk=256):
    n, width = q.shape
    m = k.shape[0]
    lo, hi = block_range(q_ids, k_ids, bq, bk)
    pairs = width // LANES
    col = lambda rows: pl.BlockSpec((rows, LANES), lambda i, *_: (0, i))
    whole = lambda rows: pl.BlockSpec((rows, LANES), lambda i, *_: (0, 0))
    out, lse = pl.pallas_call(
        functools.partial(attend_kernel, causal, bq, bk),
        out_shape=(jax.ShapeDtypeStruct((n, width), BF16), jax.ShapeDtypeStruct((n, width), F32)),
        grid_spec=pltpu.PrefetchScalarGridSpec(
            num_scalar_prefetch=2,
            grid=(pairs,),
            in_specs=[col(n), col(m), col(m), whole(n), whole(m)],
            out_specs=[col(n), col(n)],
        ),
        compiler_params=pltpu.CompilerParams(vmem_limit_bytes=VMEM_LIMIT),
        cost_estimate=pl.CostEstimate(flops=int(4e9), bytes_accessed=int(12e6), transcendentals=int(4e6)),
        name="attend",
    )(lo, hi, q, k, v, fq, fk)
    lse = lse.reshape(n, pairs, LANES)[:, :, :2].transpose(1, 2, 0)
    return out, lse


def attend_back(q, k, v, g, lse, delta, q_ids, k_ids, fq, fk, causal, bq=256, bk=256):
    n, width = q.shape
    m = k.shape[0]
    lo, hi = block_range(k_ids, q_ids, bk, bq)
    pairs = width // LANES
    col = lambda rows: pl.BlockSpec((rows, LANES), lambda i, *_: (0, i))
    whole = lambda rows: pl.BlockSpec((rows, LANES), lambda i, *_: (0, 0))
    vec = pl.BlockSpec((1, 2, n), lambda i, *_: (i, 0, 0))
    return pl.pallas_call(
        functools.partial(attend_back_kernel, causal, bq, bk),
        out_shape=(
            jax.ShapeDtypeStruct((n, width), BF16),
            jax.ShapeDtypeStruct((m, width), BF16),
            jax.ShapeDtypeStruct((m, width), BF16),
        ),
        grid_spec=pltpu.PrefetchScalarGridSpec(
            num_scalar_prefetch=2,
            grid=(pairs,),
            in_specs=[col(n), col(m), col(m), whole(n), whole(m), col(n), vec, vec],
            out_specs=[col(n), col(m), col(m)],
            scratch_shapes=[pltpu.VMEM((n, LANES), F32)],
        ),
        compiler_params=pltpu.CompilerParams(vmem_limit_bytes=VMEM_LIMIT),
        cost_estimate=pl.CostEstimate(flops=int(10e9), bytes_accessed=int(12e6), transcendentals=int(4e6)),
        name="attend_back",
    )(lo, hi, q, k, v, fq, fk, g, lse, delta)


def norm_forward(summed, gain, shift):
    centred = summed - jnp.mean(summed, axis=-1, keepdims=True)
    inverse = lax.rsqrt(jnp.mean(centred * centred, axis=-1, keepdims=True) + EPSILON)
    normed = centred * inverse
    return normed * gain + shift, normed, inverse


def norm_backward(upstream, normed, inverse, gain):
    scaled = upstream * gain
    first_mean = jnp.mean(scaled, axis=-1, keepdims=True)
    second_mean = jnp.mean(scaled * normed, axis=-1, keepdims=True)
    result = inverse * (scaled - first_mean - normed * second_mean)
    return result, jnp.sum(upstream * normed, axis=0), jnp.sum(upstream, axis=0)


def head_sums(a, b):
    n, width = a.shape
    prod = (a.astype(F32) * b.astype(F32)).reshape(n, width // HDIM, HDIM)
    return jnp.sum(prod, axis=2).T.reshape(width // LANES, 2, n)


def local_step(x, e, ct, t_ids, s_ids, w, gains, shifts):
    x32 = x.astype(F32)
    q, k, v = [dot(x, w["qkv"][c], NT).astype(BF16) for c in range(3)]
    k2, v2 = [dot(e, w["ckv"][c], NT).astype(BF16) for c in range(2)]
    fq, fk = seg_features(t_ids, t_ids)
    _, fs = seg_features(t_ids, s_ids)
    ctx1, lse1 = attend(q, k, v, t_ids, t_ids, fq, fk, True)
    h1, n1, i1 = norm_forward(x32 + dot(ctx1, w["out"], NN), gains[0], shifts[0])
    h1b = h1.astype(BF16)
    q2 = dot(h1b, w["cq"], NT).astype(BF16)
    ctx2, lse2 = attend(q2, k2, v2, t_ids, s_ids, fq, fs, False)
    h2, n2, i2 = norm_forward(h1 + dot(ctx2, w["cout"], NN), gains[1], shifts[1])
    h2b = h2.astype(BF16)
    blocks = w["up"].shape[0]
    acts, slopes = [], []
    a3 = 0.0
    for b in range(blocks):
        u = dot(h2b, w["up"][b], NT)
        phi = 0.5 * (1.0 + lax.erf(u * (2 ** -0.5)))
        acts.append((u * phi).astype(BF16))
        slopes.append((phi + u * jnp.exp(-0.5 * u * u) * ((2 * jnp.pi) ** -0.5)).astype(BF16))
        a3 = a3 + dot(acts[b], w["down"][b], NN)
    h3, n3, i3 = norm_forward(h2 + a3, gains[2], shifts[2])
    layer_out = h3.astype(BF16)
    dr3, gg3, gs3 = norm_backward(ct.astype(F32), n3, i3, gains[2])
    da3 = dr3.astype(BF16)
    g_up, g_down = [], []
    dh2 = dr3
    for b in range(blocks):
        g_down.append(dot(acts[b], da3, TN).astype(BF16))
        du = (slopes[b].astype(F32) * dot(da3, w["down"][b], NT)).astype(BF16)
        g_up.append(dot(du, h2b, TN).astype(BF16))
        dh2 = dh2 + dot(du, w["up"][b], NN)
    dr2, gg2, gs2 = norm_backward(dh2, n2, i2, gains[1])
    da2 = dr2.astype(BF16)
    g_cout = dot(ctx2, da2, TN).astype(BF16)
    dctx2 = dot(da2, w["cout"], NT).astype(BF16)
    dq2, dk2, dv2 = attend_back(q2, k2, v2, dctx2, lse2, head_sums(dctx2, ctx2), t_ids, s_ids, fq, fs, False)
    g_cq = dot(dq2, h1b, TN).astype(BF16)
    g_ckv = jnp.stack([dot(dk2, e, TN), dot(dv2, e, TN)]).astype(BF16)
    grad_e = (dot(dk2, w["ckv"][0], NN) + dot(dv2, w["ckv"][1], NN)).astype(BF16)
    dh1 = dr2 + dot(dq2, w["cq"], NN)
    dr1, gg1, gs1 = norm_backward(dh1, n1, i1, gains[0])
    da1 = dr1.astype(BF16)
    g_out = dot(ctx1, da1, TN).astype(BF16)
    dctx1 = dot(da1, w["out"], NT).astype(BF16)
    dq, dk, dv = attend_back(q, k, v, dctx1, lse1, head_sums(dctx1, ctx1), t_ids, t_ids, fq, fk, True)
    g_qkv = jnp.stack([dot(dq, x, TN), dot(dk, x, TN), dot(dv, x, TN)]).astype(BF16)
    grad_x = (dr1 + dot(dq, w["qkv"][0], NN) + dot(dk, w["qkv"][1], NN) + dot(dv, w["qkv"][2], NN)).astype(BF16)
    grads = dict(qkv=g_qkv, out=g_out, cq=g_cq, ckv=g_ckv, cout=g_cout, up=jnp.stack(g_up), down=jnp.stack(g_down))
    return layer_out, grad_x, grad_e, grads, jnp.stack([gg1, gg2, gg3]), jnp.stack([gs1, gs2, gs3])


def gather_rows(shard):
    mats, rows, width = shard.shape
    dp, tensor = lax.axis_size("dp"), lax.axis_size("tensor")
    piece = mats * rows // dp
    mine = lax.dynamic_slice_in_dim(
        shard.reshape(mats * rows, width), lax.axis_index("dp") * piece, piece, 0
    )
    full = lax.all_gather(mine, ("dp", "tensor"), axis=0, tiled=True)
    full = full.reshape(mats, dp // mats, tensor, piece, width).transpose(0, 2, 1, 3, 4)
    return full.reshape(mats, tensor * rows, width)


def reduce_rows(grad):
    mats, all_rows, width = grad.shape
    dp, tensor = lax.axis_size("dp"), lax.axis_size("tensor")
    rows = all_rows // tensor
    piece = mats * rows // dp
    grad = grad.reshape(mats, tensor, dp // mats, piece, width).transpose(0, 2, 1, 3, 4)
    mine = lax.psum_scatter(
        grad.reshape(dp * tensor * piece, width), ("dp", "tensor"), scatter_dimension=0, tiled=True
    )
    return lax.all_gather(mine, "dp", axis=0, tiled=True).reshape(mats, rows, width)


def per_device(
    inputs, encoded, cotangent, tgt_seg, src_seg, self_qkv, self_out, cross_q, cross_kv, cross_out, ffn_up, ffn_down, gains, shifts
):
    me = lax.axis_index("tensor")
    t_ids = lax.dynamic_index_in_dim(tgt_seg, me, 0, keepdims=False)
    s_ids = lax.dynamic_index_in_dim(src_seg, me, 0, keepdims=False)
    pack = jnp.concatenate(
        [
            self_qkv.transpose(0, 2, 1),
            self_out[None],
            cross_q.T[None],
            cross_kv.transpose(0, 2, 1),
            cross_out[None],
        ],
        axis=0,
    )
    pack = gather_rows(pack)
    hidden = ffn_down.shape[0]
    dp, tensor = lax.axis_size("dp"), lax.axis_size("tensor")
    ffn = jnp.stack([ffn_up.T, ffn_down], axis=0)
    piece = hidden // dp
    mine = lax.dynamic_slice_in_dim(ffn, lax.axis_index("dp") * piece, piece, 1)
    ffn = lax.all_gather(mine, ("dp", "tensor"), axis=1, tiled=True)
    w = dict(
        qkv=pack[0:3], out=pack[3], cq=pack[4], ckv=pack[5:7], cout=pack[7],
        up=ffn[0].reshape(tensor, hidden, -1), down=ffn[1].reshape(tensor, hidden, -1),
    )
    layer_out, grad_x, grad_e, grads, grad_gains, grad_shifts = local_step(
        inputs, encoded, cotangent, t_ids, s_ids, w, gains, shifts
    )
    width = inputs.shape[1]
    g_ffn = jnp.stack([grads["up"].reshape(-1, width), grads["down"].reshape(-1, width)])
    g_ffn = lax.psum_scatter(g_ffn, ("dp", "tensor"), scatter_dimension=1, tiled=True)
    g_ffn = lax.all_gather(g_ffn, "dp", axis=1, tiled=True)
    g_pack = jnp.concatenate(
        [grads["qkv"], grads["out"][None], grads["cq"][None], grads["ckv"], grads["cout"][None]], axis=0
    )
    g_pack = reduce_rows(g_pack)
    g32 = g_pack.astype(F32)
    grad_gains, grad_shifts = lax.psum((grad_gains, grad_shifts), ("dp", "tensor"))
    return (
        layer_out,
        grad_x,
        grad_e,
        g32[0:3].transpose(0, 2, 1),
        g32[3],
        g32[4].T,
        g32[5:7].transpose(0, 2, 1),
        g32[7],
        g_ffn[0].astype(F32).T,
        g_ffn[1].astype(F32),
        grad_gains,
        grad_shifts,
    )


def solution(mesh):
    rows = P(("dp", "tensor"), None)
    in_specs = (
        rows, rows, rows, P("dp", None), P("dp", None),
        P(None, None, "tensor"), P("tensor", None), P(None, "tensor"), P(None, None, "tensor"), P("tensor", None),
        P(None, "tensor"), P("tensor", None), P(), P(),
    )
    out_specs = (
        rows, rows, rows,
        P(None, None, "tensor"), P("tensor", None), P(None, "tensor"), P(None, None, "tensor"), P("tensor", None),
        P(None, "tensor"), P("tensor", None), P(), P(),
    )
    return jax.shard_map(per_device, mesh=mesh, in_specs=in_specs, out_specs=out_specs, check_vma=False)
```

time: 2960 us -> 678 us (0.23)
  waiting for transfers between devices: 1910 us -> 233 us
  matrix products: 420 us -> 138 us
  local copies, waits for them, and re-layouts: 226 us -> 62.5 us
  other arithmetic: 188 us -> 39.3 us
  Pallas kernels: 0 us -> 148 us
  loops' own time: 124 us -> 0 us
    reduce_scatter x7 -> x2, waiting for transfers between devices: 974 us -> 163 us  [the longest x1 163 us: reduce_rows(): lax.psum_scatter(grad.reshape(dp * tensor * piece, width), ('dp', 'tensor...]
    all_gather x7 -> x4, waiting for transfers between devices: 791 us -> 69.4 us  [the longest x1 69.4 us: gather_rows(): full = lax.all_gather(mine, ('dp', 'tensor'), axis=0, tiled=True)]
    dot_general x133 -> x48, matrix products: 420 us -> 138 us  [dot(): return lax.dot_general(a, b, dims, preferred_element_type=F32)]
    pallas_call x0 -> x4, Pallas kernels: none -> 148 us  [the longest x2 74.7 us: attend(): pl.pallas_call(functools.partial(attend_kernel, causal, bq, bk), out_shap...]
    psum x1 -> x0, waiting for transfers between devices: 147 us -> none  [per_device(): lax.psum((grad_self_qkv, grad_self_out, grad_cross_q, grad_cross_kv, grad...]
    dynamic_slice x192 -> x4, local copies, waits for them, and re-layouts: 137 us -> 4.97 us  [the longest x2 1.89 us: per_device(): t_ids = lax.dynamic_index_in_dim(tgt_seg, me, 0, keepdims=False)]
    another operation x4 -> x0, loops' own time: 124 us -> none  [the longest x2 74.6 us: attend_back(): lax.scan(one_block, (empty, empty), jnp.arange(item_count, dtype=jnp.int32))]
    dynamic_update_slice x32 -> x0, other arithmetic: 55.6 us -> none  [the longest x16 45.7 us: one_block(): lax.dynamic_update_slice_in_dim(value_total, value_sum, row_start, 0)]
  transfers between devices with their start and end apart: 15 -> 6, of which waited for: 15 -> 2; matrix products, arithmetic and copies ran while one was open for 2% -> 22% of each run, Pallas kernels for 0% -> 22%
where the time goes in v1:
time: 678 us; the launch traced here: 677 us
  waiting for transfers between devices  233 us (34%)
  Pallas kernels  148 us (22%)
  matrix products  138 us (20%)
  local copies, waits for them, and re-layouts  62.5 us (9%)
  blocking collectives  40.6 us (6%)
  other arithmetic  39.3 us (6%)
  between operations  15.6 us (2%)
    reduce_scatter x1, waiting for transfers between devices, reduce_rows(): lax.psum_scatter(grad.reshape(dp * tensor * piece, width), ('dp', 'tensor...  163 us
    dot_general x48, matrix products, dot(): return lax.dot_general(a, b, dims, preferred_element_type=F32)  138 us
    pallas_call x2, Pallas kernels, attend(): pl.pallas_call(functools.partial(attend_kernel, causal, bq, bk), out_shap...  74.7 us
    pallas_call x2, Pallas kernels, attend_back(): pl.pallas_call(functools.partial(attend_back_kernel, causal, bq, bk), out...  73.2 us
    all_gather x1, waiting for transfers between devices, gather_rows(): full = lax.all_gather(mine, ('dp', 'tensor'), axis=0, tiled=True)  69.4 us
    psum x1, blocking collectives, per_device(): lax.psum((grad_gains, grad_shifts), ('dp', 'tensor'))  40.6 us
    unnamed x120, local copies, waits for them, and re-layouts  33.1 us
  transfers between devices with their start and end apart: 6, of which 2 were waited for; matrix products, arithmetic and copies ran while one was open for 22% of the time, Pallas kernels for 22%

profile of v1, /device:TPU:0, one launch (start us, length us, event | category | flops | bytes accessed | tf_op | source)
XLA Modules:
  0.0 677.0 jit_solution(11610236479321325131)
XLA Ops:
  31.8 69.4 %all-gather.5.cloned.1.call-done = bf16[6144,768]{1,0:T(8,128)(2,1)} async-done(((bf16[192,768]{1,0:T(8,128)(2,1)}), bf16[6144,768]{1,0:T(8,128)(2,1)}) %all-gather.5.cloned.1.call-update) | async-done | bytes 9437200 | tf_op jit(solution)/shard_map/all_gather | solution.py:282
  101.1 4.4 fusion.32.v_ref
  105.6 3.8 fusion.31.k_ref
  109.4 3.8 fusion.30.q_ref
  113.3 31.0 %attend.2 = (bf16[1024,768]{1,0:T(8,128)(2,1)}, f32[1024,768]{1,0:T(8,128)}) custom-call(s32[4]{0:T(128)} %get-tuple-element.145.lo_ref, s32[4]{0:T(128)} %get-tuple-element.144.hi_ref, bf16[1024,768]{1,0:T(8,128)(2,1)} %fusion.30.q_ref, bf16[1024,768]{1,0:T(8,128)(2,1)} %fusion.31.k_ref, bf16[1024,768]{1,0:T(8,128)(2,1)} %fusion.32.v_ref, ...), custom_call_target="tpu_custom_call" | custom-call | flops 4000000000 | bytes 12000000 | tf_op jit(solution)/shard_map/attend/pallas_call | solution.py:156
  147.9 4.5 fusion.34.v_ref
  152.4 4.2 fusion.33.k_ref
  156.6 4.2 convolution_convert_fusion.4.q_ref
  160.8 43.7 %attend.3 = (bf16[1024,768]{1,0:T(8,128)(2,1)}, f32[1024,768]{1,0:T(8,128)}) custom-call(s32[4]{0:T(128)} %get-tuple-element.143.lo_ref, s32[4]{0:T(128)} %get-tuple-element.142.hi_ref, bf16[1024,768]{1,0:T(8,128)(2,1)} %convolution_convert_fusion.4.q_ref, bf16[1024,768]{1,0:T(8,128)(2,1)} %fusion.33.k_ref, bf16[1024,768]{1,0:T(8,128)(2,1)} %fusion.34.v_ref, ...), custom_call_target="tpu_custom_call" | custom-call | flops 4000000000 | bytes 12000000 | tf_op jit(solution)/shard_map/attend/pallas_call | solution.py:156
  214.9 4.6 multiply_convert_fusion.5
  231.4 3.7 fusion.105
  272.2 8.3 %pad_maximum_fusion = bf16[2,3072,768]{2,1,0:T(8,128)(2,1)} fusion(bf16[1,3072,768]{2,1,0:T(8,128)(2,1)} %bitcast.209, bf16[1,3072,768]{2,1,0:T(8,128)(2,1)} %bitcast.208), kind=kLoop, calls=%fused_computation | loop fusion | flops 4718592 | bytes 18874368 | tf_op jit(solution)/shard_map/stack | solution.py:330
  298.1 4.9 multiply_reduce_fusion
  304.6 6.0 convert_multiply_fusion.3
  310.5 3.7 copy.113
  318.8 42.3 %attend_back.2 = (bf16[1024,768]{1,0:T(8,128)(2,1)}, bf16[1024,768]{1,0:T(8,128)(2,1)}, bf16[1024,768]{1,0:T(8,128)(2,1)}) custom-call(s32[4]{0:T(128)} %get-tuple-element.141.lo_ref, s32[4]{0:T(128)} %get-tuple-element.140.hi_ref, bf16[1024,768]{1,0:T(8,128)(2,1)} %convolution_convert_fusion.4.q_ref, bf16[1024,768]{1,0:T(8,128)(2,1)} %fusion.33.k_ref, ...), custom_call_target="tpu_custom_call" | custom-call | flops 10000000000 | bytes 12000000 | tf_op jit(solution)/shard_map/attend_back/pallas_call | solution.py:181
  361.2 4.3 multiply_reduce_fusion.1
  367.0 5.8 convert_multiply_fusion.2
  380.9 30.9 %attend_back.3 = (bf16[1024,768]{1,0:T(8,128)(2,1)}, bf16[1024,768]{1,0:T(8,128)(2,1)}, bf16[1024,768]{1,0:T(8,128)(2,1)}) custom-call(s32[4]{0:T(128)} %get-tuple-element.145.lo_ref, s32[4]{0:T(128)} %get-tuple-element.144.hi_ref, bf16[1024,768]{1,0:T(8,128)(2,1)} %fusion.30.q_ref, bf16[1024,768]{1,0:T(8,128)(2,1)} %fusion.31.k_ref, ...), custom_call_target="tpu_custom_call" | custom-call | flops 10000000000 | bytes 12000000 | tf_op jit(solution)/shard_map/attend_back/pallas_call | solution.py:181
  427.7 3.7 copy-done.16
  432.1 163.1 %reduce-scatter.3.cloned.1.call-done = bf16[192,768]{1,0:T(8,128)(2,1)} async-done(((bf16[6144,768]{1,0:T(8,128)(2,1)}), bf16[192,768]{1,0:T(8,128)(2,1)}) %reduce-scatter.3.cloned.1.call-update) | async-done | bytes 294928 | tf_op jit(solution)/shard_map/reduce_scatter | solution.py:293
  608.1 40.6 %all-reduce = (f32[3,768]{1,0:T(4,128)}, f32[3,768]{1,0:T(4,128)}) all-reduce(f32[3,768]{1,0:T(4,128)S(1)} %pad_maximum_fusion.3, f32[3,768]{1,0:T(4,128)S(1)} %pad_maximum_fusion.4), channel_id=1, replica_groups=mesh['dp'=8,'tensor'=4] {'dp','tensor'}, use_global_device_ids=true, to_apply=%region_25.26 | all-reduce | flops 4608 | bytes 36864 | tf_op jit(solution)/shard_map/psum | solution.py:338
  652.1 3.9 add_convert_fusion
  655.9 4.2 fusion.59
  (235 shorter events, 162.4 us)
Async XLA Ops:
  7.2 140.7 %copy-start = (bf16[1024,768]{1,0:T(8,128)(2,1)S(1)}, bf16[1024,768]{1,0:T(8,128)(2,1)}, u32[]{:S(2)}) copy-start(bf16[1024,768]{1,0:T(8,128)(2,1)} %param.15) | copy-start | bytes 4718596
  7.2 5.7 copy-start.29
  7.2 6.6 copy-start.30
  7.2 93.9 %all-gather.5.cloned.1.call-start = ((), (), s32[]{:S(2)}) async-start(), calls=%async_computation.2 | async-start | bytes 9732096 | tf_op jit(solution)/shard_map/all_gather | solution.py:282
  16.2 195.3 %all-gather.7.cloned.1.call-start = ((), (), s32[]{:S(2)}) async-start(), calls=%async_computation.3 | async-start | bytes 9732096 | tf_op jit(solution)/shard_map/all_gather | solution.py:321
  19.6 411.9 %reduce-scatter.5.cloned.1.call-start = ((), (), s32[]{:S(2)}) async-start(), calls=%async_computation.6 | async-start | bytes 9732096 | tf_op jit(solution)/shard_map/reduce_scatter | solution.py:331
  22.9 4.7 copy-start.31
  22.9 4.7 copy-start.32
  27.7 176.8 %copy-start.33 = (f32[768]{0:T(1024)}, f32[768]{0:T(1024)S(1)}, u32[]{:S(2)}) copy-start(f32[768]{0:T(1024)S(1)} %get-tuple-element.96) | copy-start | bytes 9220
  101.1 4.4 copy-start.20
  113.3 31.0 %copy-start.22 = (bf16[1024,768]{0,1:T(8,128)(2,1)S(1)}, bf16[1024,768]{0,1:T(8,128)(2,1)}, u32[]{:S(2)}) copy-start(bf16[1024,768]{0,1:T(8,128)(2,1)} %copy.99) | copy-start | bytes 4718596
  147.5 57.1 %copy-start.10 = (f32[1024,768]{0,1:T(8,128)}, f32[1024,768]{0,1:T(8,128)S(1)}, u32[]{:S(2)}) copy-start(f32[1024,768]{0,1:T(8,128)S(1)} %get-tuple-element.123) | copy-start | bytes 9437188
  211.6 7.9 %slice-start = ((s8[9437184]{0:T(1024)(128)(4,1)}), s8[4194304]{0:T(1024)(128)(4,1)S(1)}, s32[]{:S(2)}) async-start(s8[9437184]{0:T(1024)(128)(4,1)} %bitcast.219), calls=%async_computation.8 | async-start | bytes 8388608
  211.6 7.9 %slice-start.1 = ((s8[9437184]{0:T(1024)(128)(4,1)}), s8[4194304]{0:T(1024)(128)(4,1)S(1)}, s32[]{:S(2)}) async-start(s8[9437184]{0:T(1024)(128)(4,1)} %bitcast.219), calls=%async_computation.9 | async-start | bytes 8388608
  214.9 4.6 slice-start.2
  280.5 314.6 %reduce-scatter.3.cloned.1.call-start = ((), (), s32[]{:S(2)}) async-start(), calls=%async_computation.4 | async-start | bytes 9732096 | tf_op jit(solution)/shard_map/reduce_scatter | solution.py:293
  304.6 6.0 copy-start.13
  318.8 42.3 %copy-start.11 = (f32[1024,768]{0,1:T(8,128)S(1)}, f32[1024,768]{0,1:T(8,128)}, u32[]{:S(2)}) copy-start(f32[1024,768]{0,1:T(8,128)} %copy-done.10) | copy-start | bytes 9437188
  318.8 42.3 %copy-start.14 = (f32[1024,768]{0,1:T(8,128)S(1)}, f32[1024,768]{0,1:T(8,128)}, u32[]{:S(2)}) copy-start(f32[1024,768]{0,1:T(8,128)} %copy-done.13) | copy-start | bytes 9437188
  367.0 5.8 copy-start.6
  380.9 30.9 %copy-start.21 = (bf16[1024,768]{1,0:T(8,128)(2,1)S(1)}, bf16[1024,768]{1,0:T(8,128)(2,1)}, u32[]{:S(2)}) copy-start(bf16[1024,768]{1,0:T(8,128)(2,1)} %param.14) | copy-start | bytes 4718596
  431.4 163.8 %copy-start.17 = (bf16[1024,768]{0,1:T(8,128)(2,1)S(1)}, bf16[1024,768]{0,1:T(8,128)(2,1)}, u32[]{:S(2)}) copy-start(bf16[1024,768]{0,1:T(8,128)(2,1)} %get-tuple-element.117) | copy-start | bytes 4718596
  431.4 224.5 %all-gather.11.cloned.1.call-start = ((), (), s32[]{:S(2)}) async-start(), calls=%async_computation.7 | async-start | bytes 2654208 | tf_op jit(solution)/shard_map/all_gather | solution.py:332
  432.0 231.1 %all-gather.9.cloned.1.call-start = ((), (), s32[]{:S(2)}) async-start(), calls=%async_computation.5 | async-start | bytes 2654208 | tf_op jit(solution)/shard_map/all_gather | solution.py:296
  (37 other events, 90.5 us)
Sparse Core Ops, SparseCore 0:
  16.4 84.7 all-gather.4
  104.8 80.6 all-gather.6
  280.6 148.0 reduce-scatter.4
  435.5 159.6 reduce-scatter.2
  596.9 28.2 all-gather.10
  626.9 29.2 all-gather.8
